TPU v7x, 32 devices: a whole 2x2x4 slice. The times are simulated.
32 devices in a mesh: groups: 2 (over y), mem: 4 (over z), head: 2 (over x), pair: 2 (over core).
Axes of the slice: x: 2, y: 2, z: 4, core: 2. Of those that a mesh axis runs over, the one named last changes fastest.
Arguments:
- queries: bfloat16 [384, 4096], P(('groups', 'mem', 'pair'), 'head'), parts along dimension 0, may hold values from -17 to 17
- row_question: int32 [384], P(('groups', 'mem', 'pair')), parts along dimension 0, may hold values from 0 to 3
- keys: bfloat16 [8192, 4096], P(('groups', 'mem'), 'head'), parts along dimension 0, may hold values from -6 to 6
- values: bfloat16 [8192, 4096], P(('groups', 'mem'), 'head'), parts along dimension 0, may hold values from -6 to 6
- lengths: int32 [16], P(('groups', 'mem')), parts along dimension 0, may hold values from 64 to 512
- passage_question: int32 [16], P(('groups', 'mem')), parts along dimension 0, may hold values from 0 to 3, as said below
Outputs:
- attended: bfloat16 [384, 4096], P(('groups', 'mem', 'pair'), 'head'), parts along dimension 0
There are 2 independent parts, one for each index of `groups`. A program takes and returns all parts, laid end to end along the dimension named above; each array names one. Nothing has to cross between parts.
Inputs may be any that keep to these rules, and one draw needn't show every extreme that they name: `passage_question`: every question of 0 to 3 owns at least one passage.
All inputs are finite; a program needn't handle non-finite values.
Results may differ from a plain program's by a relative error of at most 0.013.
Values may be sent and summed in bfloat16 or wider, within the bound.
A program may use at most 64 MiB of HBM per device.

v0:
```python
import jax
import jax.numpy as jnp
from jax import lax
from jax.sharding import PartitionSpec as P

DH = 64


NEG = -1e30


def passed_along(block, axis, distance):
    devices = range(lax.axis_size(axis))
    route = [((i - distance) % len(devices), i) for i in devices]
    return lax.ppermute(block, axis, route)


def update(query_rows, row_quest, maxima, totals, accumulated, keys, values, tok_quest, tok_live):
    row_count = query_rows.shape[0]
    head_count = maxima.shape[1]
    query_heads = query_rows.reshape(row_count, head_count, DH)
    key_heads = keys.reshape(-1, head_count, DH)
    value_heads = values.reshape(-1, head_count, DH)
    scores = jnp.einsum("rhd,thd->rht", query_heads, key_heads, preferred_element_type=jnp.float32)
    usable = (row_quest[:, None] == tok_quest[None, :]) & tok_live[None, :]
    scores = jnp.where(usable[:, None, :], scores, NEG)
    new_max = jnp.maximum(maxima, jnp.max(scores, axis=2))
    weights = jnp.where(usable[:, None, :], jnp.exp(scores - new_max[:, :, None]), 0.0)
    factor = jnp.exp(maxima - new_max)
    totals = totals * factor + jnp.sum(weights, axis=2)
    mixture = jnp.einsum(
        "rht,thd->rhd",
        weights.astype(jnp.bfloat16),
        value_heads,
        preferred_element_type=jnp.float32,
    )
    accumulated = (
        accumulated.reshape(row_count, head_count, DH) * factor[:, :, None] + mixture
    ).reshape(row_count, head_count * DH)
    return (new_max, totals, accumulated)


def body(queries, row_question, keys, values, lengths, passage_question):
    pass_count = lengths.shape[0]
    slot_count = keys.shape[0] // pass_count
    positions = lax.broadcasted_iota(jnp.int32, (pass_count, slot_count), 1)
    tok_live = (positions < lengths[:, None]).reshape(-1)
    tok_quest = (
        jnp.broadcast_to(passage_question[:, None], (pass_count, slot_count))
        .reshape(-1)
        .astype(jnp.float32)
    )
    row_count = queries.shape[0]
    head_count = keys.shape[1] // DH
    cycle_size = lax.axis_size("mem")
    row_quest = row_question.astype(jnp.float32)
    start_max = jnp.full((row_count, head_count), NEG, jnp.float32)
    start_total = jnp.zeros((row_count, head_count), jnp.float32)
    start_acc = jnp.zeros((row_count, head_count * DH), jnp.float32)

    def single_turn(turn_index, carry):
        moving_rows, moving_quest, maxima, totals, accumulated = carry
        maxima, totals, accumulated = update(
            moving_rows,
            moving_quest,
            maxima,
            totals,
            accumulated,
            keys,
            values,
            tok_quest,
            tok_live,
        )
        moving_rows = passed_along(moving_rows, "mem", 1)
        moving_quest, maxima, totals, accumulated = (
            passed_along(moving_quest.astype(jnp.bfloat16), "mem", 1).astype(moving_quest.dtype),
            passed_along(maxima.astype(jnp.bfloat16), "mem", 1).astype(maxima.dtype),
            passed_along(totals.astype(jnp.bfloat16), "mem", 1).astype(totals.dtype),
            passed_along(accumulated.astype(jnp.bfloat16), "mem", 1).astype(accumulated.dtype),
        )
        return (moving_rows, moving_quest, maxima, totals, accumulated)

    final = lax.fori_loop(
        0, cycle_size, single_turn, (queries, row_quest, start_max, start_total, start_acc)
    )
    totals = final[3]
    accumulated = final[4]
    result = accumulated.reshape(row_count, head_count, DH) / totals[:, :, None]
    return result.reshape(row_count, head_count * DH).astype(jnp.bfloat16)


def solution(mesh):
    in_specs = (
        P(("groups", "mem", "pair"), "head"),
        P(("groups", "mem", "pair")),
        P(("groups", "mem"), "head"),
        P(("groups", "mem"), "head"),
        P(("groups", "mem")),
        P(("groups", "mem")),
    )
    out_specs = P(("groups", "mem", "pair"), "head")
    return jax.shard_map(body, mesh=mesh, in_specs=in_specs, out_specs=out_specs, check_vma=False)
```

profile of v0, /device:TPU:0, one launch (start us, length us, event | category | flops | bytes accessed | tf_op | source)
XLA Modules:
  0.0 84.3 jit_solution(13260291695658346015)
XLA Ops:
  0.0 6.4 %copy.14 = bf16[1024,2048]{0,1:T(8,128)(2,1)} copy(bf16[1024,2048]{1,0:T(8,128)(2,1)} %param.10) | data formatting | bytes 8388608
  6.4 6.5 %copy.15 = bf16[1024,2048]{0,1:T(8,128)(2,1)} copy(bf16[1024,2048]{1,0:T(8,128)(2,1)} %param.11) | data formatting | bytes 8388608
  13.0 70.2 %while.19 = (s32[]{:T(128)}, bf16[24,2048]{1,0:T(8,128)(2,1)S(1)}, f32[24]{0:T(128)S(1)}, f32[24,32]{0,1:T(8,128)S(1)}, f32[24,32]{0,1:T(8,128)S(1)}, /*index=5*...) while((s32[]{:T(128)}, bf16[24,2048]{1,0:T(8,128)(2,1)S(1)}, ...), condition=%wide.region_3.4_spmd.clone, body=%wide.region_0.3_spmd.clone.sunk | while | flops 209493808 | bytes 37834676 | solution.py:83
  13.7 3.2 %fusion.42 = (f32[24,32]{0,1:T(8,128)S(1)}, f32[32,1024,24]{1,2,0:T(8,128)S(1)}) fusion(pred[24,1024]{1,0:T(8,128)(4,1)S(1)} %compare_and_fusion.2, bf16[1024,32,64]{0,2,1:T(8,128)(2,1)} %bitcast.50, bf16[24,32,64]{2,1,0:T(8,128)(2,1)S(1)} %reshape.68), kind=kOutput, calls=%fused_computation.4.clone.1 | convolution fusion | flops 102235392 | bytes 7465984 | tf_op jit(solution)/shard_map/while/body/eval_jaxpr/rhd,thd->rht/dot_general | solution.py:24
  16.9 0.8 fusion.44
  17.8 1.7 %fusion.46 = bf16[24,32,64]{2,0,1:T(8,128)(2,1)S(1)} fusion(bf16[1024,32,64]{0,2,1:T(8,128)(2,1)S(1)} %bitcast.51, f32[32,1024,24]{1,2,0:T(8,128)S(1)} %get-tuple-element.214, f32[24,32]{0,1:T(8,128)S(1)} %get-tuple-element.215, pred[24,1024]{1,0:T(8,128)(4,1)S(1)} %compare_and_fusion.2, f32[24,32,64]{2,1,0:T(8,128)S(1)} %reshape.69, ...), kind=kOutput, calls=%fused_computation.14.clone.1 | convolution fusion | flops 103956480 | bytes 7665664 | tf_op jit(solution)/shard_map/while/body/eval_jaxpr/rht,thd->rhd/dot_general | solution.py:31
  19.8 3.1 %collective-permute-start.4 = (bf16[24,2048]{1,0:T(8,128)(2,1)S(1)}, bf16[24,2048]{1,0:T(8,128)(2,1)S(1)}, u32[]{:S(2)}, u32[]{:S(2)}) collective-permute-start(bf16[24,2048]{1,0:T(8,128)(2,1)S(1)} %convert_element_type.91), channel_id=1, source_target_pairs={{12,0},{0,4},{4,8},{8,12},{13,1},{1,5},{5,9},{9,13},{14,2},{2,6},{... | collective-permute-start | bytes 294920 | tf_op jit(solution)/shard_map/while/body/eval_jaxpr/ppermute | solution.py:15
  22.8 1.6 %collective-permute-start = (bf16[24,2048]{1,0:T(8,128)(2,1)S(1)}, bf16[24,2048]{1,0:T(8,128)(2,1)S(1)}, u32[]{:S(2)}, u32[]{:S(2)}) collective-permute-start(bf16[24,2048]{1,0:T(8,128)(2,1)S(1)} %copy.40), channel_id=1, source_target_pairs={{12,0},{0,4},{4,8},{8,12},{13,1},{1,5},{5,9},{9,13},{14,2},{2,6},{... | collective-permute-start | bytes 294920 | tf_op jit(solution)/shard_map/while/body/eval_jaxpr/ppermute | solution.py:15
  24.4 1.6 %collective-permute-start.3 = (bf16[24,32]{0,1:T(8,128)(2,1)S(1)}, bf16[24,32]{0,1:T(8,128)(2,1)S(1)}, u32[]{:S(2)}, u32[]{:S(2)}) collective-permute-start(bf16[24,32]{0,1:T(8,128)(2,1)S(1)} %get-tuple-element.216), channel_id=1, source_target_pairs={{12,0},{0,4},{4,8},{8,12},{13,1},{1,5},{5,9},{9,13},{14,2},{2,6},{... | collective-permute-start | bytes 4616 | tf_op jit(solution)/shard_map/while/body/eval_jaxpr/ppermute | solution.py:15
  26.1 1.7 %collective-permute-start.1 = (bf16[24]{0:T(256)(128)(2,1)S(1)}, bf16[24]{0:T(256)(128)(2,1)S(1)}, u32[]{:S(2)}, u32[]{:S(2)}) collective-permute-start(bf16[24]{0:T(256)(128)(2,1)S(1)} %convert_element_type.87), channel_id=1, source_target_pairs={{12,0},{0,4},{4,8},{8,12},{13,1},{1,5},{5,9},{9,13},{14,2},{2,6},{... | collective-permute-start | bytes 152 | tf_op jit(solution)/shard_map/while/body/eval_jaxpr/ppermute | solution.py:15
  27.8 3.7 %collective-permute-done.1 = bf16[24]{0:T(256)(128)(2,1)S(1)} collective-permute-done((bf16[24]{0:T(256)(128)(2,1)S(1)}, bf16[24]{0:T(256)(128)(2,1)S(1)}, u32[]{:S(2)}, u32[]{:S(2)}) %collective-permute-start.1) | collective-permute-done | bytes 80 | tf_op jit(solution)/shard_map/while/body/eval_jaxpr/ppermute | solution.py:15
  32.3 3.2 %fusion.42 = (f32[24,32]{0,1:T(8,128)S(1)}, f32[32,1024,24]{1,2,0:T(8,128)S(1)}) fusion(pred[24,1024]{1,0:T(8,128)(4,1)S(1)} %compare_and_fusion.2, bf16[1024,32,64]{0,2,1:T(8,128)(2,1)} %bitcast.50, bf16[24,32,64]{2,1,0:T(8,128)(2,1)S(1)} %reshape.68), kind=kOutput, calls=%fused_computation.4.clone.1 | convolution fusion | flops 102235392 | bytes 7465984 | tf_op jit(solution)/shard_map/while/body/eval_jaxpr/rhd,thd->rht/dot_general | solution.py:24
  35.5 0.8 fusion.44
  36.4 1.7 %fusion.46 = bf16[24,32,64]{2,0,1:T(8,128)(2,1)S(1)} fusion(bf16[1024,32,64]{0,2,1:T(8,128)(2,1)S(1)} %bitcast.51, f32[32,1024,24]{1,2,0:T(8,128)S(1)} %get-tuple-element.214, f32[24,32]{0,1:T(8,128)S(1)} %get-tuple-element.215, pred[24,1024]{1,0:T(8,128)(4,1)S(1)} %compare_and_fusion.2, f32[24,32,64]{2,1,0:T(8,128)S(1)} %reshape.69, ...), kind=kOutput, calls=%fused_computation.14.clone.1 | convolution fusion | flops 103956480 | bytes 7665664 | tf_op jit(solution)/shard_map/while/body/eval_jaxpr/rht,thd->rhd/dot_general | solution.py:31
  38.4 1.4 %collective-permute-start = (bf16[24,2048]{1,0:T(8,128)(2,1)S(1)}, bf16[24,2048]{1,0:T(8,128)(2,1)S(1)}, u32[]{:S(2)}, u32[]{:S(2)}) collective-permute-start(bf16[24,2048]{1,0:T(8,128)(2,1)S(1)} %copy.40), channel_id=1, source_target_pairs={{12,0},{0,4},{4,8},{8,12},{13,1},{1,5},{5,9},{9,13},{14,2},{2,6},{... | collective-permute-start | bytes 294920 | tf_op jit(solution)/shard_map/while/body/eval_jaxpr/ppermute | solution.py:15
  39.8 1.6 %collective-permute-start.3 = (bf16[24,32]{0,1:T(8,128)(2,1)S(1)}, bf16[24,32]{0,1:T(8,128)(2,1)S(1)}, u32[]{:S(2)}, u32[]{:S(2)}) collective-permute-start(bf16[24,32]{0,1:T(8,128)(2,1)S(1)} %get-tuple-element.216), channel_id=1, source_target_pairs={{12,0},{0,4},{4,8},{8,12},{13,1},{1,5},{5,9},{9,13},{14,2},{2,6},{... | collective-permute-start | bytes 4616 | tf_op jit(solution)/shard_map/while/body/eval_jaxpr/ppermute | solution.py:15
  41.4 2.0 %collective-permute-start.2 = (bf16[24,32]{0,1:T(8,128)(2,1)S(1)}, bf16[24,32]{0,1:T(8,128)(2,1)S(1)}, u32[]{:S(2)}, u32[]{:S(2)}) collective-permute-start(bf16[24,32]{0,1:T(8,128)(2,1)S(1)} %get-tuple-element.213), channel_id=1, source_target_pairs={{12,0},{0,4},{4,8},{8,12},{13,1},{1,5},{5,9},{9,13},{14,2},{2,6},{... | collective-permute-start | bytes 4616 | tf_op jit(solution)/shard_map/while/body/eval_jaxpr/ppermute | solution.py:15
  43.4 5.3 %collective-permute-done.1 = bf16[24]{0:T(256)(128)(2,1)S(1)} collective-permute-done((bf16[24]{0:T(256)(128)(2,1)S(1)}, bf16[24]{0:T(256)(128)(2,1)S(1)}, u32[]{:S(2)}, u32[]{:S(2)}) %collective-permute-start.1) | collective-permute-done | bytes 80 | tf_op jit(solution)/shard_map/while/body/eval_jaxpr/ppermute | solution.py:15
  49.5 3.2 %fusion.42 = (f32[24,32]{0,1:T(8,128)S(1)}, f32[32,1024,24]{1,2,0:T(8,128)S(1)}) fusion(pred[24,1024]{1,0:T(8,128)(4,1)S(1)} %compare_and_fusion.2, bf16[1024,32,64]{0,2,1:T(8,128)(2,1)} %bitcast.50, bf16[24,32,64]{2,1,0:T(8,128)(2,1)S(1)} %reshape.68), kind=kOutput, calls=%fused_computation.4.clone.1 | convolution fusion | flops 102235392 | bytes 7465984 | tf_op jit(solution)/shard_map/while/body/eval_jaxpr/rhd,thd->rht/dot_general | solution.py:24
  52.7 0.8 fusion.44
  53.6 1.7 %fusion.46 = bf16[24,32,64]{2,0,1:T(8,128)(2,1)S(1)} fusion(bf16[1024,32,64]{0,2,1:T(8,128)(2,1)S(1)} %bitcast.51, f32[32,1024,24]{1,2,0:T(8,128)S(1)} %get-tuple-element.214, f32[24,32]{0,1:T(8,128)S(1)} %get-tuple-element.215, pred[24,1024]{1,0:T(8,128)(4,1)S(1)} %compare_and_fusion.2, f32[24,32,64]{2,1,0:T(8,128)S(1)} %reshape.69, ...), kind=kOutput, calls=%fused_computation.14.clone.1 | convolution fusion | flops 103956480 | bytes 7665664 | tf_op jit(solution)/shard_map/while/body/eval_jaxpr/rht,thd->rhd/dot_general | solution.py:31
  55.7 1.1 %collective-permute-start.3 = (bf16[24,32]{0,1:T(8,128)(2,1)S(1)}, bf16[24,32]{0,1:T(8,128)(2,1)S(1)}, u32[]{:S(2)}, u32[]{:S(2)}) collective-permute-start(bf16[24,32]{0,1:T(8,128)(2,1)S(1)} %get-tuple-element.216), channel_id=1, source_target_pairs={{12,0},{0,4},{4,8},{8,12},{13,1},{1,5},{5,9},{9,13},{14,2},{2,6},{... | collective-permute-start | bytes 4616 | tf_op jit(solution)/shard_map/while/body/eval_jaxpr/ppermute | solution.py:15
  56.8 3.8 %collective-permute-start.2 = (bf16[24,32]{0,1:T(8,128)(2,1)S(1)}, bf16[24,32]{0,1:T(8,128)(2,1)S(1)}, u32[]{:S(2)}, u32[]{:S(2)}) collective-permute-start(bf16[24,32]{0,1:T(8,128)(2,1)S(1)} %get-tuple-element.213), channel_id=1, source_target_pairs={{12,0},{0,4},{4,8},{8,12},{13,1},{1,5},{5,9},{9,13},{14,2},{2,6},{... | collective-permute-start | bytes 4616 | tf_op jit(solution)/shard_map/while/body/eval_jaxpr/ppermute | solution.py:15
  60.6 5.3 %collective-permute-done.1 = bf16[24]{0:T(256)(128)(2,1)S(1)} collective-permute-done((bf16[24]{0:T(256)(128)(2,1)S(1)}, bf16[24]{0:T(256)(128)(2,1)S(1)}, u32[]{:S(2)}, u32[]{:S(2)}) %collective-permute-start.1) | collective-permute-done | bytes 80 | tf_op jit(solution)/shard_map/while/body/eval_jaxpr/ppermute | solution.py:15
  66.7 3.2 %fusion.42 = (f32[24,32]{0,1:T(8,128)S(1)}, f32[32,1024,24]{1,2,0:T(8,128)S(1)}) fusion(pred[24,1024]{1,0:T(8,128)(4,1)S(1)} %compare_and_fusion.2, bf16[1024,32,64]{0,2,1:T(8,128)(2,1)} %bitcast.50, bf16[24,32,64]{2,1,0:T(8,128)(2,1)S(1)} %reshape.68), kind=kOutput, calls=%fused_computation.4.clone.1 | convolution fusion | flops 102235392 | bytes 7465984 | tf_op jit(solution)/shard_map/while/body/eval_jaxpr/rhd,thd->rht/dot_general | solution.py:24
  69.9 0.8 fusion.44
  70.8 1.7 %fusion.46 = bf16[24,32,64]{2,0,1:T(8,128)(2,1)S(1)} fusion(bf16[1024,32,64]{0,2,1:T(8,128)(2,1)S(1)} %bitcast.51, f32[32,1024,24]{1,2,0:T(8,128)S(1)} %get-tuple-element.214, f32[24,32]{0,1:T(8,128)S(1)} %get-tuple-element.215, pred[24,1024]{1,0:T(8,128)(4,1)S(1)} %compare_and_fusion.2, f32[24,32,64]{2,1,0:T(8,128)S(1)} %reshape.69, ...), kind=kOutput, calls=%fused_computation.14.clone.1 | convolution fusion | flops 103956480 | bytes 7665664 | tf_op jit(solution)/shard_map/while/body/eval_jaxpr/rht,thd->rhd/dot_general | solution.py:31
  72.5 0.2 convert_element_type.91
  72.9 0.8 collective-permute-start.3
  73.7 4.0 %collective-permute-start.2 = (bf16[24,32]{0,1:T(8,128)(2,1)S(1)}, bf16[24,32]{0,1:T(8,128)(2,1)S(1)}, u32[]{:S(2)}, u32[]{:S(2)}) collective-permute-start(bf16[24,32]{0,1:T(8,128)(2,1)S(1)} %get-tuple-element.213), channel_id=1, source_target_pairs={{12,0},{0,4},{4,8},{8,12},{13,1},{1,5},{5,9},{9,13},{14,2},{2,6},{... | collective-permute-start | bytes 4616 | tf_op jit(solution)/shard_map/while/body/eval_jaxpr/ppermute | solution.py:15
  77.8 5.3 %collective-permute-done.1 = bf16[24]{0:T(256)(128)(2,1)S(1)} collective-permute-done((bf16[24]{0:T(256)(128)(2,1)S(1)}, bf16[24]{0:T(256)(128)(2,1)S(1)}, u32[]{:S(2)}, u32[]{:S(2)}) %collective-permute-start.1) | collective-permute-done | bytes 80 | tf_op jit(solution)/shard_map/while/body/eval_jaxpr/ppermute | solution.py:15
  83.6 0.7 divide_convert_fusion
  (120 shorter events, 4.6 us)
Async XLA Ops:
  6.4 6.6 %copy-start.3 = (s32[24]{0:T(128)S(1)}, s32[24]{0:T(128)}, u32[]{:S(2)}) copy-start(s32[24]{0:T(128)} %param.9) | copy-start | bytes 292
  6.4 6.6 %copy-start.4 = (s32[2]{0:T(128)S(1)}, s32[2]{0:T(128)}, u32[]{:S(2)}) copy-start(s32[2]{0:T(128)} %param.13) | copy-start | bytes 28
  6.4 6.6 %copy-start.1 = (bf16[24,2048]{1,0:T(8,128)(2,1)S(1)}, bf16[24,2048]{1,0:T(8,128)(2,1)}, u32[]{:S(2)}) copy-start(bf16[24,2048]{1,0:T(8,128)(2,1)} %param.8) | copy-start | bytes 294916
  6.4 6.6 %copy-start.2 = (s32[2]{0:T(128)S(1)}, s32[2]{0:T(128)}, u32[]{:S(2)}) copy-start(s32[2]{0:T(128)} %param.12) | copy-start | bytes 28
  13.7 4.1 %copy-start = (bf16[1024,2048]{0,1:T(8,128)(2,1)S(1)}, bf16[1024,2048]{0,1:T(8,128)(2,1)}, u32[]{:S(2)}) copy-start(bf16[1024,2048]{0,1:T(8,128)(2,1)} %get-tuple-element.249) | copy-start | bytes 12582916 | tf_op jit(solution)/shard_map/while
  19.8 11.8 %collective-permute-start.4 = (bf16[24,2048]{1,0:T(8,128)(2,1)S(1)}, bf16[24,2048]{1,0:T(8,128)(2,1)S(1)}, u32[]{:S(2)}, u32[]{:S(2)}) collective-permute-start(bf16[24,2048]{1,0:T(8,128)(2,1)S(1)} %convert_element_type.91), channel_id=1, source_target_pairs={{12,0},{0,4},{4,8},{8,12},{13,1},{1,5},{5,9},{9,13},{14,2},{2,6},{... | collective-permute-start | bytes 294920 | tf_op jit(solution)/shard_map/while/body/eval_jaxpr/ppermute | solution.py:15
  22.8 8.7 %collective-permute-start = (bf16[24,2048]{1,0:T(8,128)(2,1)S(1)}, bf16[24,2048]{1,0:T(8,128)(2,1)S(1)}, u32[]{:S(2)}, u32[]{:S(2)}) collective-permute-start(bf16[24,2048]{1,0:T(8,128)(2,1)S(1)} %copy.40), channel_id=1, source_target_pairs={{12,0},{0,4},{4,8},{8,12},{13,1},{1,5},{5,9},{9,13},{14,2},{2,6},{... | collective-permute-start | bytes 294920 | tf_op jit(solution)/shard_map/while/body/eval_jaxpr/ppermute | solution.py:15
  24.4 7.1 %collective-permute-start.3 = (bf16[24,32]{0,1:T(8,128)(2,1)S(1)}, bf16[24,32]{0,1:T(8,128)(2,1)S(1)}, u32[]{:S(2)}, u32[]{:S(2)}) collective-permute-start(bf16[24,32]{0,1:T(8,128)(2,1)S(1)} %get-tuple-element.216), channel_id=1, source_target_pairs={{12,0},{0,4},{4,8},{8,12},{13,1},{1,5},{5,9},{9,13},{14,2},{2,6},{... | collective-permute-start | bytes 4616 | tf_op jit(solution)/shard_map/while/body/eval_jaxpr/ppermute | solution.py:15
  26.0 5.5 %collective-permute-start.2 = (bf16[24,32]{0,1:T(8,128)(2,1)S(1)}, bf16[24,32]{0,1:T(8,128)(2,1)S(1)}, u32[]{:S(2)}, u32[]{:S(2)}) collective-permute-start(bf16[24,32]{0,1:T(8,128)(2,1)S(1)} %get-tuple-element.213), channel_id=1, source_target_pairs={{12,0},{0,4},{4,8},{8,12},{13,1},{1,5},{5,9},{9,13},{14,2},{2,6},{... | collective-permute-start | bytes 4616 | tf_op jit(solution)/shard_map/while/body/eval_jaxpr/ppermute | solution.py:15
  26.1 5.4 %collective-permute-start.1 = (bf16[24]{0:T(256)(128)(2,1)S(1)}, bf16[24]{0:T(256)(128)(2,1)S(1)}, u32[]{:S(2)}, u32[]{:S(2)}) collective-permute-start(bf16[24]{0:T(256)(128)(2,1)S(1)} %convert_element_type.87), channel_id=1, source_target_pairs={{12,0},{0,4},{4,8},{8,12},{13,1},{1,5},{5,9},{9,13},{14,2},{2,6},{... | collective-permute-start | bytes 152 | tf_op jit(solution)/shard_map/while/body/eval_jaxpr/ppermute | solution.py:15
  32.3 4.1 %copy-start = (bf16[1024,2048]{0,1:T(8,128)(2,1)S(1)}, bf16[1024,2048]{0,1:T(8,128)(2,1)}, u32[]{:S(2)}) copy-start(bf16[1024,2048]{0,1:T(8,128)(2,1)} %get-tuple-element.249) | copy-start | bytes 12582916 | tf_op jit(solution)/shard_map/while
  38.4 10.4 %collective-permute-start.4 = (bf16[24,2048]{1,0:T(8,128)(2,1)S(1)}, bf16[24,2048]{1,0:T(8,128)(2,1)S(1)}, u32[]{:S(2)}, u32[]{:S(2)}) collective-permute-start(bf16[24,2048]{1,0:T(8,128)(2,1)S(1)} %convert_element_type.91), channel_id=1, source_target_pairs={{12,0},{0,4},{4,8},{8,12},{13,1},{1,5},{5,9},{9,13},{14,2},{2,6},{... | collective-permute-start | bytes 294920 | tf_op jit(solution)/shard_map/while/body/eval_jaxpr/ppermute | solution.py:15
  38.4 10.4 %collective-permute-start = (bf16[24,2048]{1,0:T(8,128)(2,1)S(1)}, bf16[24,2048]{1,0:T(8,128)(2,1)S(1)}, u32[]{:S(2)}, u32[]{:S(2)}) collective-permute-start(bf16[24,2048]{1,0:T(8,128)(2,1)S(1)} %copy.40), channel_id=1, source_target_pairs={{12,0},{0,4},{4,8},{8,12},{13,1},{1,5},{5,9},{9,13},{14,2},{2,6},{... | collective-permute-start | bytes 294920 | tf_op jit(solution)/shard_map/while/body/eval_jaxpr/ppermute | solution.py:15
  39.8 8.9 %collective-permute-start.3 = (bf16[24,32]{0,1:T(8,128)(2,1)S(1)}, bf16[24,32]{0,1:T(8,128)(2,1)S(1)}, u32[]{:S(2)}, u32[]{:S(2)}) collective-permute-start(bf16[24,32]{0,1:T(8,128)(2,1)S(1)} %get-tuple-element.216), channel_id=1, source_target_pairs={{12,0},{0,4},{4,8},{8,12},{13,1},{1,5},{5,9},{9,13},{14,2},{2,6},{... | collective-permute-start | bytes 4616 | tf_op jit(solution)/shard_map/while/body/eval_jaxpr/ppermute | solution.py:15
  41.4 7.3 %collective-permute-start.2 = (bf16[24,32]{0,1:T(8,128)(2,1)S(1)}, bf16[24,32]{0,1:T(8,128)(2,1)S(1)}, u32[]{:S(2)}, u32[]{:S(2)}) collective-permute-start(bf16[24,32]{0,1:T(8,128)(2,1)S(1)} %get-tuple-element.213), channel_id=1, source_target_pairs={{12,0},{0,4},{4,8},{8,12},{13,1},{1,5},{5,9},{9,13},{14,2},{2,6},{... | collective-permute-start | bytes 4616 | tf_op jit(solution)/shard_map/while/body/eval_jaxpr/ppermute | solution.py:15
  43.4 5.3 %collective-permute-start.1 = (bf16[24]{0:T(256)(128)(2,1)S(1)}, bf16[24]{0:T(256)(128)(2,1)S(1)}, u32[]{:S(2)}, u32[]{:S(2)}) collective-permute-start(bf16[24]{0:T(256)(128)(2,1)S(1)} %convert_element_type.87), channel_id=1, source_target_pairs={{12,0},{0,4},{4,8},{8,12},{13,1},{1,5},{5,9},{9,13},{14,2},{2,6},{... | collective-permute-start | bytes 152 | tf_op jit(solution)/shard_map/while/body/eval_jaxpr/ppermute | solution.py:15
  49.5 4.1 %copy-start = (bf16[1024,2048]{0,1:T(8,128)(2,1)S(1)}, bf16[1024,2048]{0,1:T(8,128)(2,1)}, u32[]{:S(2)}) copy-start(bf16[1024,2048]{0,1:T(8,128)(2,1)} %get-tuple-element.249) | copy-start | bytes 12582916 | tf_op jit(solution)/shard_map/while
  55.6 10.4 %collective-permute-start.4 = (bf16[24,2048]{1,0:T(8,128)(2,1)S(1)}, bf16[24,2048]{1,0:T(8,128)(2,1)S(1)}, u32[]{:S(2)}, u32[]{:S(2)}) collective-permute-start(bf16[24,2048]{1,0:T(8,128)(2,1)S(1)} %convert_element_type.91), channel_id=1, source_target_pairs={{12,0},{0,4},{4,8},{8,12},{13,1},{1,5},{5,9},{9,13},{14,2},{2,6},{... | collective-permute-start | bytes 294920 | tf_op jit(solution)/shard_map/while/body/eval_jaxpr/ppermute | solution.py:15
  55.6 10.4 %collective-permute-start = (bf16[24,2048]{1,0:T(8,128)(2,1)S(1)}, bf16[24,2048]{1,0:T(8,128)(2,1)S(1)}, u32[]{:S(2)}, u32[]{:S(2)}) collective-permute-start(bf16[24,2048]{1,0:T(8,128)(2,1)S(1)} %copy.40), channel_id=1, source_target_pairs={{12,0},{0,4},{4,8},{8,12},{13,1},{1,5},{5,9},{9,13},{14,2},{2,6},{... | collective-permute-start | bytes 294920 | tf_op jit(solution)/shard_map/while/body/eval_jaxpr/ppermute | solution.py:15
  55.7 10.2 %collective-permute-start.3 = (bf16[24,32]{0,1:T(8,128)(2,1)S(1)}, bf16[24,32]{0,1:T(8,128)(2,1)S(1)}, u32[]{:S(2)}, u32[]{:S(2)}) collective-permute-start(bf16[24,32]{0,1:T(8,128)(2,1)S(1)} %get-tuple-element.216), channel_id=1, source_target_pairs={{12,0},{0,4},{4,8},{8,12},{13,1},{1,5},{5,9},{9,13},{14,2},{2,6},{... | collective-permute-start | bytes 4616 | tf_op jit(solution)/shard_map/while/body/eval_jaxpr/ppermute | solution.py:15
  56.8 9.1 %collective-permute-start.2 = (bf16[24,32]{0,1:T(8,128)(2,1)S(1)}, bf16[24,32]{0,1:T(8,128)(2,1)S(1)}, u32[]{:S(2)}, u32[]{:S(2)}) collective-permute-start(bf16[24,32]{0,1:T(8,128)(2,1)S(1)} %get-tuple-element.213), channel_id=1, source_target_pairs={{12,0},{0,4},{4,8},{8,12},{13,1},{1,5},{5,9},{9,13},{14,2},{2,6},{... | collective-permute-start | bytes 4616 | tf_op jit(solution)/shard_map/while/body/eval_jaxpr/ppermute | solution.py:15
  60.6 5.3 %collective-permute-start.1 = (bf16[24]{0:T(256)(128)(2,1)S(1)}, bf16[24]{0:T(256)(128)(2,1)S(1)}, u32[]{:S(2)}, u32[]{:S(2)}) collective-permute-start(bf16[24]{0:T(256)(128)(2,1)S(1)} %convert_element_type.87), channel_id=1, source_target_pairs={{12,0},{0,4},{4,8},{8,12},{13,1},{1,5},{5,9},{9,13},{14,2},{2,6},{... | collective-permute-start | bytes 152 | tf_op jit(solution)/shard_map/while/body/eval_jaxpr/ppermute | solution.py:15
  66.7 4.1 %copy-start = (bf16[1024,2048]{0,1:T(8,128)(2,1)S(1)}, bf16[1024,2048]{0,1:T(8,128)(2,1)}, u32[]{:S(2)}) copy-start(bf16[1024,2048]{0,1:T(8,128)(2,1)} %get-tuple-element.249) | copy-start | bytes 12582916 | tf_op jit(solution)/shard_map/while
  72.8 10.4 %collective-permute-start.4 = (bf16[24,2048]{1,0:T(8,128)(2,1)S(1)}, bf16[24,2048]{1,0:T(8,128)(2,1)S(1)}, u32[]{:S(2)}, u32[]{:S(2)}) collective-permute-start(bf16[24,2048]{1,0:T(8,128)(2,1)S(1)} %convert_element_type.91), channel_id=1, source_target_pairs={{12,0},{0,4},{4,8},{8,12},{13,1},{1,5},{5,9},{9,13},{14,2},{2,6},{... | collective-permute-start | bytes 294920 | tf_op jit(solution)/shard_map/while/body/eval_jaxpr/ppermute | solution.py:15
  72.8 10.4 %collective-permute-start = (bf16[24,2048]{1,0:T(8,128)(2,1)S(1)}, bf16[24,2048]{1,0:T(8,128)(2,1)S(1)}, u32[]{:S(2)}, u32[]{:S(2)}) collective-permute-start(bf16[24,2048]{1,0:T(8,128)(2,1)S(1)} %copy.40), channel_id=1, source_target_pairs={{12,0},{0,4},{4,8},{8,12},{13,1},{1,5},{5,9},{9,13},{14,2},{2,6},{... | collective-permute-start | bytes 294920 | tf_op jit(solution)/shard_map/while/body/eval_jaxpr/ppermute | solution.py:15
  72.9 10.2 %collective-permute-start.3 = (bf16[24,32]{0,1:T(8,128)(2,1)S(1)}, bf16[24,32]{0,1:T(8,128)(2,1)S(1)}, u32[]{:S(2)}, u32[]{:S(2)}) collective-permute-start(bf16[24,32]{0,1:T(8,128)(2,1)S(1)} %get-tuple-element.216), channel_id=1, source_target_pairs={{12,0},{0,4},{4,8},{8,12},{13,1},{1,5},{5,9},{9,13},{14,2},{2,6},{... | collective-permute-start | bytes 4616 | tf_op jit(solution)/shard_map/while/body/eval_jaxpr/ppermute | solution.py:15
  73.7 9.4 %collective-permute-start.2 = (bf16[24,32]{0,1:T(8,128)(2,1)S(1)}, bf16[24,32]{0,1:T(8,128)(2,1)S(1)}, u32[]{:S(2)}, u32[]{:S(2)}) collective-permute-start(bf16[24,32]{0,1:T(8,128)(2,1)S(1)} %get-tuple-element.213), channel_id=1, source_target_pairs={{12,0},{0,4},{4,8},{8,12},{13,1},{1,5},{5,9},{9,13},{14,2},{2,6},{... | collective-permute-start | bytes 4616 | tf_op jit(solution)/shard_map/while/body/eval_jaxpr/ppermute | solution.py:15
  77.8 5.3 %collective-permute-start.1 = (bf16[24]{0:T(256)(128)(2,1)S(1)}, bf16[24]{0:T(256)(128)(2,1)S(1)}, u32[]{:S(2)}, u32[]{:S(2)}) collective-permute-start(bf16[24]{0:T(256)(128)(2,1)S(1)} %convert_element_type.87), channel_id=1, source_target_pairs={{12,0},{0,4},{4,8},{8,12},{13,1},{1,5},{5,9},{9,13},{14,2},{2,6},{... | collective-permute-start | bytes 152 | tf_op jit(solution)/shard_map/while/body/eval_jaxpr/ppermute | solution.py:15
where the time goes:
time: 84.6 us; the launch traced here: 84.3 us
  starting transfers between devices  23.2 us (27%)
  matrix products  19.7 us (23%)
  waiting for transfers between devices  19.6 us (23%)
  local copies, waits for them, and re-layouts  16.1 us (19%)
  other arithmetic  5.01 us (6%)
    ppermute x20, starting transfers between devices, passed_along(): return lax.ppermute(block, axis, route)  23.2 us
    ppermute x20, waiting for transfers between devices, passed_along(): return lax.ppermute(block, axis, route)  19.6 us
    unnamed x10, local copies, waits for them, and re-layouts  12.9 us
    dot_general x4, matrix products, update(): jnp.einsum('rhd,thd->rht', query_heads, key_heads, preferred_element_type...  12.8 us
    dot_general x4, matrix products, update(): jnp.einsum('rht,thd->rhd', weights.astype(jnp.bfloat16), value_heads, pre...  6.9 us
    reduce_sum x4, other arithmetic, update(): totals = totals * factor + jnp.sum(weights, axis=2)  3.36 us
  transfers between devices with their start and end apart: 20, of which 4 were waited for; matrix products, arithmetic and copies ran while one was open for 0% of the time, Pallas kernels for 0%

commit v1 on v0

v1 whole, which is shorter than its diff:
```python
import functools

import jax
import jax.numpy as jnp
from jax import lax
from jax.experimental import pallas as pl
from jax.experimental.pallas import tpu as pltpu
from jax.sharding import PartitionSpec as P

DH = 64
LANES = 256
PACK = LANES // DH
TOP = 16
NEG = -1e30
MESH = pl.DeviceIdType.MESH


def kernel(
    n, rows, groups, slots,
    q_ref, quest_ref, k_hbm, v_hbm, len_ref, pq_ref, out_ref,
    qbuf, obuf, rbuf, stat, rstat, bias, onehot, kbuf, vbuf,
    k_sem, v_sem, qs_sem, qr_sem, os_sem, or_sem, ss_sem, sr_sem,
):
    me = lax.axis_index("mem")
    chunks = groups // 2
    both = 2 * rows
    block = min(n, 4)
    tokens = kbuf.shape[0]
    width = 2 * LANES

    def load(c, hbm, buf, sem):
        cols = pl.ds(pl.multiple_of(c * width, width), width)
        return pltpu.make_async_copy(hbm.at[:, cols], buf.at[:, cols], sem.at[c])

    for c in range(chunks):
        load(c, k_hbm, kbuf, k_sem).start()
        load(c, v_hbm, vbuf, v_sem).start()

    barrier = pltpu.get_barrier_semaphore()
    for k in range(1, n):
        pl.semaphore_signal(barrier, inc=1, device_id={"mem": lax.rem(me + k, n)}, device_id_type=MESH)

    onehot[...] = jnp.zeros_like(onehot)
    ids = lax.broadcasted_iota(jnp.int32, (TOP, rows), 0)
    onehot[:, :rows] = jnp.where(ids == quest_ref[...], 1.0, 0.0)
    qbuf[me, 0:TOP, :] = onehot[...].astype(jnp.bfloat16)
    for c in range(chunks):
        halves = [
            q_ref[:, (2 * c + g) * LANES : (2 * c + g + 1) * LANES].astype(jnp.float32) for g in range(2)
        ]
        qbuf[me, TOP + both * c : TOP + both * (c + 1), :] = jnp.concatenate(halves, 0).astype(jnp.bfloat16)

    pl.semaphore_wait(barrier, n - 1)

    def query_copy(k, c, slot):
        span = pl.ds(0, TOP + both) if c == 0 else pl.ds(TOP + both * c, both)
        return pltpu.make_async_remote_copy(
            src_ref=qbuf.at[slot, span],
            dst_ref=qbuf.at[slot, span],
            send_sem=qs_sem.at[k, c],
            recv_sem=qr_sem.at[k, c],
            device_id={"mem": lax.rem(me + k, n)},
            device_id_type=MESH,
        )

    def result_copy(k, c, there, here):
        span = pl.ds(pl.multiple_of(both * c, 16), both)
        return pltpu.make_async_remote_copy(
            src_ref=obuf.at[there, span],
            dst_ref=rbuf.at[here, span],
            send_sem=os_sem.at[k, c],
            recv_sem=or_sem.at[k, c],
            device_id={"mem": lax.rem(me + k, n)},
            device_id_type=MESH,
        )

    def stat_copy(k, there, here):
        return pltpu.make_async_remote_copy(
            src_ref=stat.at[there],
            dst_ref=rstat.at[here],
            send_sem=ss_sem.at[k],
            recv_sem=sr_sem.at[k],
            device_id={"mem": lax.rem(me + k, n)},
            device_id_type=MESH,
        )

    for c in range(chunks):
        for k in range(1, n):
            query_copy(k, c, me).start()

    quest = lax.broadcasted_iota(jnp.int32, (TOP, tokens), 0)
    slot = lax.broadcasted_iota(jnp.int32, (TOP, tokens), 1)
    table = jnp.full((TOP, tokens), NEG, jnp.float32)
    for p in range(tokens // slots):
        good = (slot >= p * slots) & (slot < p * slots + len_ref[p]) & (quest == pq_ref[p])
        table = jnp.where(good, 0.0, table)
    table = table.astype(jnp.bfloat16)
    stat[...] = jnp.zeros_like(stat)

    lane_head = lax.broadcasted_iota(jnp.int32, (1, LANES), 1) // DH
    lane = lax.broadcasted_iota(jnp.int32, (1, 128), 1)

    for c in range(chunks):
        load(c, k_hbm, kbuf, k_sem).wait()
        load(c, v_hbm, vbuf, v_sem).wait()
        for k in range(1, n):
            query_copy(k, c, lax.rem(me + n - k, n)).wait_recv()

        def some(b, _, c=c):
            if c == 0:
                seen = [
                    jnp.transpose(qbuf[b * block + s, 0:TOP, 0:128].astype(jnp.float32))[:rows]
                    for s in range(block)
                ]
                bias[b] = jnp.dot(
                    jnp.concatenate(seen, 0).astype(jnp.bfloat16), table, preferred_element_type=jnp.float32
                )
            pair = [
                qbuf[b * block + s, TOP + both * c : TOP + both * (c + 1), :].astype(jnp.float32)
                for s in range(block)
            ]
            made = []
            found = [stat[b * block + s] for s in range(block)]
            for g in range(2):
                cols = slice((2 * c + g) * LANES, (2 * c + g + 1) * LANES)
                q4 = jnp.concatenate([x[g * rows : (g + 1) * rows] for x in pair], 0)
                spread = jnp.concatenate([jnp.where(lane_head == h, q4, 0.0) for h in range(PACK)], 0)
                scores = lax.dot_general(
                    spread.astype(jnp.bfloat16), kbuf[:, cols], (((1,), (1,)), ((), ())),
                    preferred_element_type=jnp.float32,
                )
                scores = scores.reshape(PACK, block * rows, tokens) + bias[b][None]
                maxima = jnp.max(scores, axis=2, keepdims=True)
                weights = jnp.exp(scores - maxima)
                totals = jnp.sum(weights, axis=2, keepdims=True)
                mixture = jnp.dot(
                    weights.astype(jnp.bfloat16).reshape(PACK * block * rows, tokens), vbuf[:, cols],
                    preferred_element_type=jnp.float32,
                ).reshape(PACK, block * rows, LANES)
                mixture = mixture / totals
                picked = mixture[0]
                for h in range(1, PACK):
                    picked = jnp.where(lane_head == h, mixture[h], picked)
                made.append(picked)
                for h in range(PACK):
                    at = (2 * c + g) * PACK + h
                    for s in range(block):
                        part = slice(s * rows, (s + 1) * rows)
                        found[s] = jnp.where(lane == at, maxima[h, part], found[s])
                        found[s] = jnp.where(lane == 64 + at, totals[h, part], found[s])
            for s in range(block):
                part = slice(s * rows, (s + 1) * rows)
                stat[b * block + s] = found[s]
                obuf[b * block + s, both * c : both * (c + 1), :] = jnp.concatenate(
                    [made[0][part], made[1][part]], 0
                ).astype(jnp.bfloat16)
            return 0

        if n == block:
            some(0, 0)
        else:
            lax.fori_loop(0, n // block, some, 0)
        if c == chunks - 1:
            for k in range(1, n):
                stat_copy(k, lax.rem(me + k, n), me).start()
        for k in range(1, n):
            result_copy(k, c, lax.rem(me + k, n), me).start()

    rstat[me] = stat[me]
    for c in range(chunks):
        span = slice(both * c, both * (c + 1))
        rbuf[me, span, :] = obuf[me, span, :]

    for k in range(1, n):
        stat_copy(k, me, lax.rem(me + n - k, n)).wait_recv()
    top = rstat[0]
    for s in range(1, n):
        top = jnp.maximum(top, rstat[s])
    shares = []
    for s in range(n):
        now = rstat[s]
        shares.append(jnp.exp(now - top) * pltpu.roll(now, 64, 1))
    whole = functools.reduce(lambda a, b: a + b, shares)
    shares = [jnp.where(lane < groups * PACK, x / whole, 0.0) for x in shares]
    shares = jnp.concatenate(shares, 0)
    high = shares.astype(jnp.bfloat16)
    low = (shares - high.astype(jnp.float32)).astype(jnp.bfloat16)
    at_head = lax.broadcasted_iota(jnp.int32, (128, LANES), 0)
    at_lane = lax.broadcasted_iota(jnp.int32, (128, LANES), 1) // DH
    for c in range(chunks):
        for k in range(1, n):
            result_copy(k, c, me, lax.rem(me + n - k, n)).wait_recv()
        factor = []
        for g in range(2):
            expand = jnp.where(at_head == (2 * c + g) * PACK + at_lane, 1.0, 0.0).astype(jnp.bfloat16)
            factor.append(
                jnp.dot(high, expand, preferred_element_type=jnp.float32)
                + jnp.dot(low, expand, preferred_element_type=jnp.float32)
            )
        sums = [0.0, 0.0]
        for s in range(n):
            got = rbuf[s, both * c : both * (c + 1), :].astype(jnp.float32)
            for g in range(2):
                sums[g] = sums[g] + got[g * rows : (g + 1) * rows] * factor[g][s * rows : (s + 1) * rows]
        for g in range(2):
            out_ref[:, (2 * c + g) * LANES : (2 * c + g + 1) * LANES] = sums[g].astype(jnp.bfloat16)

    for k in range(1, n):
        for c in range(chunks):
            query_copy(k, c, me).wait_send()
            result_copy(k, c, lax.rem(me + k, n), me).wait_send()
        stat_copy(k, lax.rem(me + k, n), me).wait_send()


def body(n, queries, row_question, keys, values, lengths, passage_question):
    rows, width = queries.shape
    tokens = keys.shape[0]
    groups = width // LANES
    chunks = groups // 2
    block = min(n, 4)
    bf16, f32 = jnp.bfloat16, jnp.float32
    vmem = pl.BlockSpec(memory_space=pltpu.VMEM)
    smem = pl.BlockSpec(memory_space=pltpu.SMEM)
    anywhere = pl.BlockSpec(memory_space=pl.ANY)
    return pl.pallas_call(
        functools.partial(kernel, n, rows, groups, tokens // lengths.shape[0]),
        out_shape=jax.ShapeDtypeStruct((rows, width), bf16),
        in_specs=[vmem, vmem, anywhere, anywhere, smem, smem],
        out_specs=vmem,
        scratch_shapes=[
            pltpu.VMEM((n, TOP + groups * rows, LANES), bf16),
            pltpu.VMEM((n, groups * rows, LANES), bf16),
            pltpu.VMEM((n, groups * rows, LANES), bf16),
            pltpu.VMEM((n, rows, 128), f32),
            pltpu.VMEM((n, rows, 128), f32),
            pltpu.VMEM((n // block, block * rows, tokens), f32),
            pltpu.VMEM((TOP, LANES), f32),
            pltpu.VMEM((tokens, width), bf16),
            pltpu.VMEM((tokens, width), bf16),
            pltpu.SemaphoreType.DMA((chunks,)),
            pltpu.SemaphoreType.DMA((chunks,)),
            pltpu.SemaphoreType.DMA((n, chunks)),
            pltpu.SemaphoreType.DMA((n, chunks)),
            pltpu.SemaphoreType.DMA((n, chunks)),
            pltpu.SemaphoreType.DMA((n, chunks)),
            pltpu.SemaphoreType.DMA((n,)),
            pltpu.SemaphoreType.DMA((n,)),
        ],
        compiler_params=pltpu.CompilerParams(
            collective_id=0, has_side_effects=True, vmem_limit_bytes=44 * 1024 * 1024
        ),
        cost_estimate=pl.CostEstimate(
            flops=4 * n * rows * width * tokens,
            bytes_accessed=4 * tokens * width,
            transcendentals=n * rows * tokens * (width // DH),
        ),
    )(queries, row_question.reshape(1, rows), keys, values, lengths, passage_question)


def solution(mesh):
    in_specs = (
        P(("groups", "mem", "pair"), "head"),
        P(("groups", "mem", "pair")),
        P(("groups", "mem"), "head"),
        P(("groups", "mem"), "head"),
        P(("groups", "mem")),
        P(("groups", "mem")),
    )
    out_specs = P(("groups", "mem", "pair"), "head")
    return jax.shard_map(
        functools.partial(body, mesh.shape["mem"]), mesh=mesh, in_specs=in_specs, out_specs=out_specs,
        check_vma=False,
    )
```

time: 84.6 us -> 36 us (0.43)
  Pallas kernels: 0 us -> 27.9 us
  starting transfers between devices: 23.2 us -> 0 us
  matrix products: 19.7 us -> 0 us
  waiting for transfers between devices: 19.6 us -> 0 us
  local copies, waits for them, and re-layouts: 16.1 us -> 7.87 us
  other arithmetic: 5.01 us -> 0 us
    pallas_call x0 -> x1, Pallas kernels: none -> 27.9 us  [body(): pl.pallas_call(functools.partial(kernel, n, rows, groups, tokens // lengt...]
    ppermute x20 -> x0, starting transfers between devices: 23.2 us -> none  [passed_along(): return lax.ppermute(block, axis, route)]
    dot_general x8 -> x0, matrix products: 19.7 us -> none  [the longest x4 12.8 us: update(): jnp.einsum('rhd,thd->rht', query_heads, key_heads, preferred_element_type...]
    ppermute x20 -> x0, waiting for transfers between devices: 19.6 us -> none  [passed_along(): return lax.ppermute(block, axis, route)]
    unnamed x10 -> x13, local copies, waits for them, and re-layouts: 12.9 us -> 7.87 us
    reduce_sum x4 -> x0, other arithmetic: 3.36 us -> none  [update(): totals = totals * factor + jnp.sum(weights, axis=2)]
    reshape x8 -> x0, local copies, waits for them, and re-layouts: 1.36 us -> none  [the longest x4 0.72 us: update(): query_heads = query_rows.reshape(row_count, head_count, DH)]
    convert_element_type x8 -> x0, local copies, waits for them, and re-layouts: 1.02 us -> none  [single_turn(): accumulated.astype(jnp.bfloat16)]
  transfers between devices with their start and end apart: 20 -> 0, of which waited for: 4 -> 0; matrix products, arithmetic and copies ran while one was open for 0% -> 0% of each run, Pallas kernels for 0% -> 0%
where the time goes in v1:
time: 36 us; the launch traced here: 35.8 us
  Pallas kernels  27.9 us (78%)
  local copies, waits for them, and re-layouts  7.87 us (22%)
    pallas_call x1, Pallas kernels, body(): pl.pallas_call(functools.partial(kernel, n, rows, groups, tokens // lengt...  27.9 us
    unnamed x13, local copies, waits for them, and re-layouts  7.87 us

profile of v1, /device:TPU:0, one launch (start us, length us, event | category | flops | bytes accessed | tf_op | source)
XLA Modules:
  0.0 35.8 jit_solution(6159499914800719293)
XLA Ops:
  0.0 0.0 copy-start
  0.0 2.2 %copy-done = bf16[1024,2048]{1,0:T(8,128)(2,1)S(1)} copy-done((bf16[1024,2048]{1,0:T(8,128)(2,1)S(1)}, bf16[1024,2048]{1,0:T(8,128)(2,1)}, u32[]{:S(2)}) %copy-start) | copy-done | bytes 4194328
  2.2 0.0 copy-start.1
  2.2 2.2 %copy-done.1 = bf16[1024,2048]{1,0:T(8,128)(2,1)S(1)} copy-done((bf16[1024,2048]{1,0:T(8,128)(2,1)S(1)}, bf16[1024,2048]{1,0:T(8,128)(2,1)}, u32[]{:S(2)}) %copy-start.1) | copy-done | bytes 4194328
  4.4 0.0 copy-start.2
  4.4 0.9 %copy-done.2 = bf16[24,2048]{1,0:T(8,128)(2,1)S(1)} copy-done((bf16[24,2048]{1,0:T(8,128)(2,1)S(1)}, bf16[24,2048]{1,0:T(8,128)(2,1)}, u32[]{:S(2)}) %copy-start.2) | copy-done | bytes 98328
  5.3 0.0 copy-start.3
  5.3 0.7 %copy-done.3 = s32[24]{0:T(128)S(1)} copy-done((s32[24]{0:T(128)S(1)}, s32[24]{0:T(128)}, u32[]{:S(2)}) %copy-start.3) | copy-done | bytes 120
  5.9 0.0 copy-start.4
  5.9 0.7 %copy-done.4 = s32[2]{0:T(128)S(1)} copy-done((s32[2]{0:T(128)S(1)}, s32[2]{0:T(128)}, u32[]{:S(2)}) %copy-start.4) | copy-done | bytes 32
  6.6 0.0 copy-start.5
  6.6 0.7 %copy-done.5 = s32[2]{0:T(128)S(1)} copy-done((s32[2]{0:T(128)S(1)}, s32[2]{0:T(128)}, u32[]{:S(2)}) %copy-start.5) | copy-done | bytes 32
  7.2 27.9 %shard_map.64 = bf16[24,2048]{1,0:T(8,128)(2,1)S(1)} custom-call(bf16[24,2048]{1,0:T(8,128)(2,1)S(1)} %copy-done.2, s32[1,24]{1,0:T(1,128)S(1)} %bitcast.1, bf16[1024,2048]{1,0:T(8,128)(2,1)S(1)} %copy-done, bf16[1024,2048]{1,0:T(8,128)(2,1)S(1)} %copy-done.1, s32[2]{0:T(128)S(1)} %copy-done.4, s32[2]{0:T(128)S(1)} %copy-done.5), custom_call_target="tpu_custom_call" | custom-call | flops 805306368 | bytes 8388608 | tf_op jit(solution)/shard_map/pallas_call | solution.py:225
  35.2 0.6 %copy.8 = bf16[24,2048]{1,0:T(8,128)(2,1)} copy(bf16[24,2048]{1,0:T(8,128)(2,1)S(1)} %shard_map.64) | data formatting | bytes 196608
Async XLA Ops:
  0.0 2.2 %copy-start = (bf16[1024,2048]{1,0:T(8,128)(2,1)S(1)}, bf16[1024,2048]{1,0:T(8,128)(2,1)}, u32[]{:S(2)}) copy-start(bf16[1024,2048]{1,0:T(8,128)(2,1)} %k_hbm.1) | copy-start | bytes 12582916
  2.2 2.2 %copy-start.1 = (bf16[1024,2048]{1,0:T(8,128)(2,1)S(1)}, bf16[1024,2048]{1,0:T(8,128)(2,1)}, u32[]{:S(2)}) copy-start(bf16[1024,2048]{1,0:T(8,128)(2,1)} %v_hbm.1) | copy-start | bytes 12582916
  4.4 0.9 %copy-start.2 = (bf16[24,2048]{1,0:T(8,128)(2,1)S(1)}, bf16[24,2048]{1,0:T(8,128)(2,1)}, u32[]{:S(2)}) copy-start(bf16[24,2048]{1,0:T(8,128)(2,1)} %q_ref.1) | copy-start | bytes 294916
  5.3 0.7 %copy-start.3 = (s32[24]{0:T(128)S(1)}, s32[24]{0:T(128)}, u32[]{:S(2)}) copy-start(s32[24]{0:T(128)} %param.7) | copy-start | bytes 292
  5.9 0.7 %copy-start.4 = (s32[2]{0:T(128)S(1)}, s32[2]{0:T(128)}, u32[]{:S(2)}) copy-start(s32[2]{0:T(128)} %len_ref.1) | copy-start | bytes 28
  6.6 0.7 %copy-start.5 = (s32[2]{0:T(128)S(1)}, s32[2]{0:T(128)}, u32[]{:S(2)}) copy-start(s32[2]{0:T(128)} %pq_ref.1) | copy-start | bytes 28

commit v2 on v1

--- a/solution.py
+++ b/solution.py
@@ -247,7 +247,7 @@
             pltpu.SemaphoreType.DMA((n,)),
         ],
         compiler_params=pltpu.CompilerParams(
-            collective_id=0, has_side_effects=True, vmem_limit_bytes=44 * 1024 * 1024
+            collective_id=0, has_side_effects=True, vmem_limit_bytes=60 * 1024 * 1024
         ),
         cost_estimate=pl.CostEstimate(
             flops=4 * n * rows * width * tokens,

time: 36 us -> 29.5 us (0.82)
  local copies, waits for them, and re-layouts: 7.87 us -> 1.54 us
    unnamed x13 -> x1, local copies, waits for them, and re-layouts: 7.87 us -> 1.54 us
where the time goes in v2:
time: 29.5 us; the launch traced here: 29.4 us
  Pallas kernels  27.8 us (94%)
  local copies, waits for them, and re-layouts  1.54 us (5%)
    pallas_call x1, Pallas kernels, body(): pl.pallas_call(functools.partial(kernel, n, rows, groups, tokens // lengt...  27.8 us
    unnamed x1, local copies, waits for them, and re-layouts  1.54 us

profile of v2, /device:TPU:0, one launch (start us, length us, event | category | flops | bytes accessed | tf_op | source)
XLA Modules:
  0.0 29.4 jit_solution(6436144752358401366)
XLA Ops:
  0.0 27.8 %shard_map.64 = bf16[24,2048]{1,0:T(8,128)(2,1)} custom-call(bf16[24,2048]{1,0:T(8,128)(2,1)} %q_ref.1, s32[1,24]{1,0:T(1,128)} %bitcast.1, bf16[1024,2048]{1,0:T(8,128)(2,1)} %k_hbm.1, bf16[1024,2048]{1,0:T(8,128)(2,1)} %v_hbm.1, s32[2]{0:T(128)} %len_ref.1, s32[2]{0:T(128)} %pq_ref.1), custom_call_target="tpu_custom_call" | custom-call | flops 805306368 | bytes 8388608 | tf_op jit(solution)/shard_map/pallas_call | solution.py:225
  27.8 1.5 %copy.8 = bf16[24,2048]{1,0:T(8,128)(2,1)} copy(bf16[24,2048]{1,0:T(8,128)(2,1)} %shard_map.64) | data formatting | bytes 196608

commit v3 on v2

--- a/solution.py
+++ b/solution.py
@@ -63,6 +63,26 @@
             device_id_type=MESH,
         )
 
+    def relay(c):
+        span = pl.ds(0, TOP + both) if c == 0 else pl.ds(TOP + both * c, both)
+        place = qbuf.at[lax.rem(me + n - 2, n), span]
+        return pltpu.make_async_remote_copy(
+            src_ref=place,
+            dst_ref=place,
+            send_sem=qs_sem.at[0, c],
+            recv_sem=qr_sem.at[lax.rem(2 * me - 1 + n, n), c],
+            device_id={"mem": lax.rem(3 * (me - 1) + 3 * n, n)},
+            device_id_type=MESH,
+        )
+
+    def pass_on(c):
+        if n == 4:
+            query_copy(2, c, lax.rem(me + n - 2, n)).wait_recv()
+
+            @pl.when((me == 1) | (me == 2))
+            def _():
+                relay(c).start()
+
     def result_copy(k, c, there, here):
         span = pl.ds(pl.multiple_of(both * c, 16), both)
         return pltpu.make_async_remote_copy(
@@ -85,8 +105,14 @@
         )
 
     for c in range(chunks):
-        for k in range(1, n):
-            query_copy(k, c, me).start()
+        for k in [n // 2] + [x for x in range(1, n) if x != n // 2]:
+            if n == 4 and k != 2:
+
+                @pl.when(jnp.abs(me - lax.rem(me + k, n)) != 3)
+                def _(k=k, c=c):
+                    query_copy(k, c, me).start()
+            else:
+                query_copy(k, c, me).start()
 
     quest = lax.broadcasted_iota(jnp.int32, (TOP, tokens), 0)
     slot = lax.broadcasted_iota(jnp.int32, (TOP, tokens), 1)
@@ -103,8 +129,13 @@
     for c in range(chunks):
         load(c, k_hbm, kbuf, k_sem).wait()
         load(c, v_hbm, vbuf, v_sem).wait()
+        if c == 0:
+            pass_on(0)
+        if c + 1 < chunks:
+            pass_on(c + 1)
         for k in range(1, n):
-            query_copy(k, c, lax.rem(me + n - k, n)).wait_recv()
+            if n != 4 or k != 2:
+                query_copy(k, c, lax.rem(me + n - k, n)).wait_recv()
 
         def some(b, _, c=c):
             if c == 0:
@@ -163,7 +194,7 @@
         if c == chunks - 1:
             for k in range(1, n):
                 stat_copy(k, lax.rem(me + k, n), me).start()
-        for k in range(1, n):
+        for k in [n // 2] + [x for x in range(1, n) if x != n // 2]:
             result_copy(k, c, lax.rem(me + k, n), me).start()
 
     rstat[me] = stat[me]
@@ -207,7 +238,20 @@
 
     for k in range(1, n):
         for c in range(chunks):
-            query_copy(k, c, me).wait_send()
+            if n == 4 and k != 2:
+
+                @pl.when(jnp.abs(me - lax.rem(me + k, n)) != 3)
+                def _(k=k, c=c):
+                    query_copy(k, c, me).wait_send()
+
+            else:
+                query_copy(k, c, me).wait_send()
+            if n == 4 and k == 2:
+
+                @pl.when((me == 1) | (me == 2))
+                def _(c=c):
+                    relay(c).wait_send()
+
             result_copy(k, c, lax.rem(me + k, n), me).wait_send()
         stat_copy(k, lax.rem(me + k, n), me).wait_send()
 

time: 29.5 us -> 28.4 us (0.963)
  Pallas kernels: 27.8 us -> 26.7 us
    pallas_call x1, Pallas kernels: 27.8 us -> 26.7 us  [body(): pl.pallas_call(functools.partial(kernel, n, rows, groups, tokens // lengt...]
where the time goes in v3:
time: 28.4 us; the launch traced here: 28.3 us
  Pallas kernels  26.7 us (94%)
  local copies, waits for them, and re-layouts  1.54 us (5%)
    pallas_call x1, Pallas kernels, body(): pl.pallas_call(functools.partial(kernel, n, rows, groups, tokens // lengt...  26.7 us
    unnamed x1, local copies, waits for them, and re-layouts  1.54 us

profile of v3, /device:TPU:0, one launch (start us, length us, event | category | flops | bytes accessed | tf_op | source)
XLA Modules:
  0.0 28.3 jit_solution(317708717224666302)
XLA Ops:
  0.0 26.7 %shard_map.64 = bf16[24,2048]{1,0:T(8,128)(2,1)} custom-call(bf16[24,2048]{1,0:T(8,128)(2,1)} %q_ref.1, s32[1,24]{1,0:T(1,128)} %bitcast.1, bf16[1024,2048]{1,0:T(8,128)(2,1)} %k_hbm.1, bf16[1024,2048]{1,0:T(8,128)(2,1)} %v_hbm.1, s32[2]{0:T(128)} %len_ref.1, s32[2]{0:T(128)} %pq_ref.1), custom_call_target="tpu_custom_call" | custom-call | flops 805306368 | bytes 8388608 | tf_op jit(solution)/shard_map/pallas_call | solution.py:269
  26.7 1.5 %copy.8 = bf16[24,2048]{1,0:T(8,128)(2,1)} copy(bf16[24,2048]{1,0:T(8,128)(2,1)} %shard_map.64) | data formatting | bytes 196608

commit v4 on v3

--- a/solution.py
+++ b/solution.py
@@ -131,8 +131,6 @@
         load(c, v_hbm, vbuf, v_sem).wait()
         if c == 0:
             pass_on(0)
-        if c + 1 < chunks:
-            pass_on(c + 1)
         for k in range(1, n):
             if n != 4 or k != 2:
                 query_copy(k, c, lax.rem(me + n - k, n)).wait_recv()
@@ -153,6 +151,8 @@
             made = []
             found = [stat[b * block + s] for s in range(block)]
             for g in range(2):
+                if g == 1 and n == 4 and c + 1 < chunks:
+                    pass_on(c + 1)
                 cols = slice((2 * c + g) * LANES, (2 * c + g + 1) * LANES)
                 q4 = jnp.concatenate([x[g * rows : (g + 1) * rows] for x in pair], 0)
                 spread = jnp.concatenate([jnp.where(lane_head == h, q4, 0.0) for h in range(PACK)], 0)

time: 28.4 us -> 30.2 us (1.063)
  Pallas kernels: 26.7 us -> 28.4 us
    pallas_call x1, Pallas kernels: 26.7 us -> 28.4 us  [body(): pl.pallas_call(functools.partial(kernel, n, rows, groups, tokens // lengt...]
where the time goes in v4:
time: 30.2 us; the launch traced here: 30 us
  Pallas kernels  28.4 us (94%)
  local copies, waits for them, and re-layouts  1.54 us (5%)
    pallas_call x1, Pallas kernels, body(): pl.pallas_call(functools.partial(kernel, n, rows, groups, tokens // lengt...  28.4 us
    unnamed x1, local copies, waits for them, and re-layouts  1.54 us

profile of v4, /device:TPU:0, one launch (start us, length us, event | category | flops | bytes accessed | tf_op | source)
XLA Modules:
  0.0 30.0 jit_solution(7904885276484097504)
XLA Ops:
  0.0 28.4 %shard_map.64 = bf16[24,2048]{1,0:T(8,128)(2,1)} custom-call(bf16[24,2048]{1,0:T(8,128)(2,1)} %q_ref.1, s32[1,24]{1,0:T(1,128)} %bitcast.1, bf16[1024,2048]{1,0:T(8,128)(2,1)} %k_hbm.1, bf16[1024,2048]{1,0:T(8,128)(2,1)} %v_hbm.1, s32[2]{0:T(128)} %len_ref.1, s32[2]{0:T(128)} %pq_ref.1), custom_call_target="tpu_custom_call" | custom-call | flops 805306368 | bytes 8388608 | tf_op jit(solution)/shard_map/pallas_call | solution.py:269
  28.4 1.5 %copy.8 = bf16[24,2048]{1,0:T(8,128)(2,1)} copy(bf16[24,2048]{1,0:T(8,128)(2,1)} %shard_map.64) | data formatting | bytes 196608
